TPU v7x, 512 devices: a whole 4x8x8 slice. The times are simulated.
512 devices in a mesh: ctx: 64 (over z, y), head: 8 (over x, core).
Axes of the slice: x: 4, y: 8, z: 8, core: 2. Of those that a mesh axis runs over, the one named last changes fastest.
Arguments:
- query_rows: bfloat16 [8192, 4096], P('ctx', 'head'), may hold values from -6 to 6
- key_rows: bfloat16 [8192, 4096], P('ctx', 'head'), may hold values from -6 to 6
- value_rows: bfloat16 [8192, 4096], P('ctx', 'head'), may hold values from -6 to 6
- decay_rates: float32 [8192, 32], P('ctx', 'head'), may hold values from 0 to 0.6, as said below
- beta_rates: float32 [8192, 32], P('ctx', 'head'), may hold values from 0 to 1
- level_weights: float32 [8192, 32, 7], P('ctx', 'head'), may hold values from 0.5 to 8
- out_weight: bfloat16 [4096, 4096], P('head', 'ctx'), may hold values from -0.09375 to 0.09375
Outputs:
- mixed: bfloat16 [8192, 4096], P('ctx', 'head')
Inputs may be any that keep to these rules, and one draw needn't show every extreme that they name: `decay_rates`: non-negative decay rate per token and head.
All inputs are finite; a program needn't handle non-finite values.
Results may differ from a plain program's by a relative error of at most 0.017.
Values may be sent and summed in bfloat16 or wider, within the bound.
A program may use at most 64 MiB of HBM per device.

v0:
```python
import jax
import jax.numpy as jnp
from jax import lax
from jax.sharding import PartitionSpec as P

DK = 128
CH = 64


topmost_level = lax.Precision.HIGHEST


def partner(value, axis, apart):
    return lax.ppermute(value, axis, [(i, i ^ 1 << apart) for i in range(lax.axis_size(axis))])


def unit_rows(vectors):
    return vectors * lax.rsqrt(jnp.sum(vectors * vectors, axis=-1, keepdims=True) + 1e-06)


def span_terms(queries, key_vecs, value_vecs, decay_vals, beta_vals):
    length = queries.shape[-2]
    key_width = queries.shape[-1]
    lower_ones = jnp.tril(jnp.ones((length, length), jnp.float32))
    inside = lower_ones > 0.5
    strict = jnp.tril(jnp.ones((length, length), jnp.float32), -1) > 0.5
    cumulative = -jnp.einsum("...s,ts->...t", decay_vals, lower_ones, precision=topmost_level)
    growth = jnp.exp(cumulative)
    gap_matrix = cumulative[..., :, None] - cumulative[..., None, :]
    ratios = jnp.where(inside, jnp.exp(jnp.minimum(gap_matrix, 0.0)), 0.0)
    key_key = jnp.einsum("...td,...sd->...ts", key_vecs, key_vecs, precision=topmost_level)
    query_key = jnp.einsum("...td,...sd->...ts", queries, key_vecs, precision=topmost_level)
    coupling = jnp.where(strict, beta_vals[..., :, None] * ratios * key_key, 0.0)
    system = coupling + jnp.eye(length, dtype=jnp.float32)
    right_side = jnp.concatenate(
        [(beta_vals * growth)[..., None] * key_vecs, beta_vals[..., None] * value_vecs], axis=-1
    )
    solved = jax.scipy.linalg.solve_triangular(system, right_side, lower=True, unit_diagonal=True)
    weight_rows = solved[..., :key_width]
    updates = solved[..., key_width:]
    scores = query_key * ratios
    inner_out = jnp.einsum("...ts,...sv->...tv", scores, updates, precision=topmost_level)
    moved_queries = growth[..., None] * queries - jnp.einsum(
        "...ts,...sk->...tk", scores, weight_rows, precision=topmost_level
    )
    final_log = cumulative[..., -1:]
    tail_keys = jnp.exp(final_log - cumulative)[..., None] * key_vecs
    transition = jnp.exp(final_log)[..., None] * jnp.eye(key_width, dtype=jnp.float32) - jnp.einsum(
        "...sk,...sj->...kj", tail_keys, weight_rows, precision=topmost_level
    )
    injection = jnp.einsum("...sk,...sv->...kv", tail_keys, updates, precision=topmost_level)
    return (transition, injection, moved_queries, inner_out)


def block_terms(queries, key_vecs, value_vecs, decay_vals, beta_vals):
    transition, injection, moved_queries, inner_out = span_terms(
        queries, key_vecs, value_vecs, decay_vals, beta_vals
    )
    key_width = queries.shape[-1]
    batch_shape = transition.shape[:-3]
    start_map = jnp.broadcast_to(
        jnp.eye(key_width, dtype=jnp.float32), batch_shape + (key_width, key_width)
    )
    start_add = jnp.zeros(batch_shape + (key_width, value_vecs.shape[-1]), jnp.float32)

    def advance(carried_pair, span_items):
        prefix_map, prefix_add = carried_pair
        span_map, span_add, span_queries, span_inner = span_items
        local_out = span_inner + jnp.einsum(
            "...tk,...kv->...tv", span_queries, prefix_add, precision=topmost_level
        )
        raised_values = jnp.einsum(
            "...tk,...kj->...tj", span_queries, prefix_map, precision=topmost_level
        )
        next_map = jnp.einsum("...ij,...jk->...ik", span_map, prefix_map, precision=topmost_level)
        next_add = (
            jnp.einsum("...ij,...jv->...iv", span_map, prefix_add, precision=topmost_level)
            + span_add
        )
        return ((next_map, next_add), (local_out, raised_values))

    span_items = (
        jnp.moveaxis(transition, -3, 0),
        jnp.moveaxis(injection, -3, 0),
        jnp.moveaxis(moved_queries, -3, 0),
        jnp.moveaxis(inner_out, -3, 0),
    )
    (block_map, block_add), (local_out, raised_values) = lax.scan(
        advance, (start_map, start_add), span_items
    )
    return (
        block_map,
        block_add,
        jnp.moveaxis(local_out, 0, -3),
        jnp.moveaxis(raised_values, 0, -3),
    )


def per_device(
    query_rows, key_rows, value_rows, decay_rates, beta_rates, level_weights, out_weight
):
    tok_rows = query_rows.shape[0]
    head_count = decay_rates.shape[1]
    level_total = level_weights.shape[2]
    sub_count = tok_rows // CH

    def heads_first(array):
        return array.reshape(sub_count, CH, head_count, DK).transpose(2, 0, 1, 3)

    queries = unit_rows(heads_first(query_rows.astype(jnp.float32)))
    key_vecs = unit_rows(heads_first(key_rows.astype(jnp.float32)))
    value_vecs = heads_first(value_rows.astype(jnp.float32))
    decay_vals = decay_rates.reshape(sub_count, CH, head_count).transpose(2, 0, 1)
    beta_vals = beta_rates.reshape(sub_count, CH, head_count).transpose(2, 0, 1)
    weight_vals = level_weights.reshape(sub_count, CH, head_count, level_total).transpose(
        2, 0, 1, 3
    )
    total_map, total_add, local_out, raised_values = block_terms(
        queries, key_vecs, value_vecs, decay_vals, beta_vals
    )
    mixed_heads = weight_vals[..., 0:1] * local_out
    position = lax.axis_index("ctx")
    level_count = lax.axis_size("ctx").bit_length() - 1
    relay_map = jnp.broadcast_to(jnp.eye(DK, dtype=jnp.float32), total_map.shape)
    for level_bit in range(level_count):
        upper_half = position // 2**level_bit % 2 == 1
        other_map, other_add = partner((total_map, total_add), "ctx", level_bit)
        fenwick_level_state = jnp.where(
            upper_half,
            jnp.einsum("hij,hjv->hiv", relay_map, other_add, precision=topmost_level),
            0.0,
        )
        relay_map = jnp.where(
            upper_half,
            jnp.einsum("hij,hjk->hik", relay_map, other_map, precision=topmost_level),
            relay_map,
        )
        first_map = jnp.where(upper_half, other_map, total_map)
        first_add = jnp.where(upper_half, other_add, total_add)
        second_map = jnp.where(upper_half, total_map, other_map)
        second_add = jnp.where(upper_half, total_add, other_add)
        total_map = jnp.einsum("hij,hjk->hik", second_map, first_map, precision=topmost_level)
        total_add = (
            jnp.einsum("hij,hjv->hiv", second_map, first_add, precision=topmost_level) + second_add
        )
        mixed_heads = mixed_heads + weight_vals[..., level_bit + 1 : level_bit + 2] * jnp.einsum(
            "mwin,mnd->mwid", raised_values, fenwick_level_state, precision=topmost_level
        )
    mixer_out = (
        mixed_heads.transpose(1, 2, 0, 3).reshape(tok_rows, head_count * DK).astype(jnp.bfloat16)
    )
    partial_value = jnp.dot(
        mixer_out,
        lax.all_gather(out_weight, "ctx", axis=1, tiled=True),
        preferred_element_type=jnp.float32,
    ).astype(jnp.bfloat16)
    summed = lax.psum_scatter(
        partial_value.astype(jnp.float32).astype(jnp.bfloat16),
        "head",
        scatter_dimension=1,
        tiled=True,
    )
    return summed


def solution(mesh):
    in_specs = (
        P("ctx", "head"),
        P("ctx", "head"),
        P("ctx", "head"),
        P("ctx", "head"),
        P("ctx", "head"),
        P("ctx", "head", None),
        P("head", "ctx"),
    )
    out_specs = P("ctx", "head")
    return jax.shard_map(
        per_device, mesh=mesh, in_specs=in_specs, out_specs=out_specs, check_vma=False
    )
```

profile of v0, /device:TPU:1, one launch (start us, length us, event | category | flops | bytes accessed | tf_op | source)
XLA Modules:
  0.0 245.2 jit_solution(4505717722166603258)
XLA Ops:
  6.5 0.7 all-gather.2.cloned.1.call-update
  7.3 0.8 reshape.69
  8.4 1.0 reshape.76
  10.0 1.0 reshape.77
  11.2 0.8 reshape.71
  12.0 0.7 fusion.48
  12.7 39.3 %custom-call.4 = f32[4,2,1,64,64]{3,4,2,1,0:T(8,128)S(1)} custom-call(f32[4,2,1,64,64]{4,3,2,1,0:T(8,128)S(1)} %fusion.48), custom_call_target="InvertDiagBlocksLowerTriangular" | custom-call | tf_op jit(solution)/shard_map/jit(_solve_triangular)/vmap(vmap())/triangular_solve | solution.py:38
  52.1 1.0 reshape.78
  53.1 0.6 convolution_multiply_fusion
  54.1 0.7 fusion.50
  55.1 1.2 convolution_bitcast_fusion.1
  56.3 0.4 fusion.43
  56.8 1.2 fusion.24
  58.1 3.2 %while.17 = (s32[]{:T(128)}, f32[4,128,128]{2,1,0:T(8,128)S(1)}, f32[4,128,128]{2,1,0:T(8,128)S(1)}, f32[2,4,64,128]{3,2,0,1:T(8,128)S(1)}, f32[2,4,64,128]{3,2,...) while((s32[]{:T(128)}, f32[4,128,128]{2,1,0:T(8,128)S(1)}, ...), condition=%wide.region_3.4_spmd.clone, body=%wide.region_2.3_spmd.clone.sunk | while | flops 302219264 | bytes 4066428 | solution.py:88
  61.3 4.0 %collective-permute-start.1 = (f32[4,128,128]{2,1,0:T(8,128)S(1)}, f32[4,128,128]{2,1,0:T(8,128)S(1)}, u32[]{:S(2)}, u32[]{:S(2)}) collective-permute-start(f32[4,128,128]{2,1,0:T(8,128)S(1)} %get-tuple-element.58), channel_id=1, source_target_pairs={{0,8},{8,0},{16,24},{24,16},{32,40},{40,32},{48,56},{56,48},{64,72... | collective-permute-start | bytes 786440 | tf_op jit(solution)/shard_map/ppermute | solution.py:14
  65.3 1.9 collective-permute-start
  67.5 1.5 collective-permute-done.1
  69.1 0.4 fusion.70
  69.5 6.3 %collective-permute-start.3 = (f32[4,128,128]{2,1,0:T(8,128)S(1)}, f32[4,128,128]{2,1,0:T(8,128)S(1)}, u32[]{:S(2)}, u32[]{:S(2)}) collective-permute-start(f32[4,128,128]{2,1,0:T(8,128)S(1)} %fusion.70), channel_id=1, source_target_pairs={{0,16},{8,24},{16,0},{24,8},{32,48},{40,56},{48,32},{56,40},{64,80... | collective-permute-start | bytes 786440 | tf_op jit(solution)/shard_map/ppermute | solution.py:14
  75.8 0.4 convolution_add_fusion.6
  76.2 9.9 %collective-permute-start.2 = (f32[4,128,128]{2,1,0:T(8,128)S(1)}, f32[4,128,128]{2,1,0:T(8,128)S(1)}, u32[]{:S(2)}, u32[]{:S(2)}) collective-permute-start(f32[4,128,128]{2,1,0:T(8,128)S(1)} %convolution_add_fusion.6), channel_id=1, source_target_pairs={{0,16},{8,24},{16,0},{24,8},{32,48},{40,56},{48,32},{56,40},{64,80... | collective-permute-start | bytes 786440 | tf_op jit(solution)/shard_map/ppermute | solution.py:14
  86.5 0.4 fusion.41
  87.3 0.4 fusion.67
  87.7 10.2 %collective-permute-start.5 = (f32[4,128,128]{2,1,0:T(8,128)S(1)}, f32[4,128,128]{2,1,0:T(8,128)S(1)}, u32[]{:S(2)}, u32[]{:S(2)}) collective-permute-start(f32[4,128,128]{2,1,0:T(8,128)S(1)} %fusion.67), channel_id=1, source_target_pairs={{0,32},{8,40},{16,48},{24,56},{32,0},{40,8},{48,16},{56,24},{64,96... | collective-permute-start | bytes 786440 | tf_op jit(solution)/shard_map/ppermute | solution.py:14
  97.9 11.8 %collective-permute-done.2 = f32[4,128,128]{2,1,0:T(8,128)S(1)} collective-permute-done((f32[4,128,128]{2,1,0:T(8,128)S(1)}, f32[4,128,128]{2,1,0:T(8,128)S(1)}, u32[]{:S(2)}, u32[]{:S(2)}) %collective-permute-start.2) | collective-permute-done | bytes 262176 | tf_op jit(solution)/shard_map/ppermute | solution.py:14
  109.8 0.4 convolution_add_fusion.5
  110.2 13.6 %collective-permute-start.4 = (f32[4,128,128]{2,1,0:T(8,128)S(1)}, f32[4,128,128]{2,1,0:T(8,128)S(1)}, u32[]{:S(2)}, u32[]{:S(2)}) collective-permute-start(f32[4,128,128]{2,1,0:T(8,128)S(1)} %convolution_add_fusion.5), channel_id=1, source_target_pairs={{0,32},{8,40},{16,48},{24,56},{32,0},{40,8},{48,16},{56,24},{64,96... | collective-permute-start | bytes 786440 | tf_op jit(solution)/shard_map/ppermute | solution.py:14
  124.2 0.4 fusion.38
  124.6 0.4 convolution_select_fusion.3
  125.0 0.4 fusion.64
  125.4 8.9 %collective-permute-start.7 = (f32[4,128,128]{2,1,0:T(8,128)S(1)}, f32[4,128,128]{2,1,0:T(8,128)S(1)}, u32[]{:S(2)}, u32[]{:S(2)}) collective-permute-start(f32[4,128,128]{2,1,0:T(8,128)S(1)} %fusion.64), channel_id=1, source_target_pairs={{0,64},{8,72},{16,80},{24,88},{32,96},{40,104},{48,112},{56,120},{... | collective-permute-start | bytes 786440 | tf_op jit(solution)/shard_map/ppermute | solution.py:14
  134.4 0.4 convolution_add_fusion.4
  134.8 8.8 %collective-permute-start.6 = (f32[4,128,128]{2,1,0:T(8,128)S(1)}, f32[4,128,128]{2,1,0:T(8,128)S(1)}, u32[]{:S(2)}, u32[]{:S(2)}) collective-permute-start(f32[4,128,128]{2,1,0:T(8,128)S(1)} %convolution_add_fusion.4), channel_id=1, source_target_pairs={{0,64},{8,72},{16,80},{24,88},{32,96},{40,104},{48,112},{56,120},{... | collective-permute-start | bytes 786440 | tf_op jit(solution)/shard_map/ppermute | solution.py:14
  144.0 0.4 fusion.35
  144.8 0.4 fusion.61
  145.2 4.7 %collective-permute-start.9 = (f32[4,128,128]{2,1,0:T(8,128)S(1)}, f32[4,128,128]{2,1,0:T(8,128)S(1)}, u32[]{:S(2)}, u32[]{:S(2)}) collective-permute-start(f32[4,128,128]{2,1,0:T(8,128)S(1)} %fusion.61), channel_id=1, source_target_pairs={{0,128},{8,136},{16,144},{24,152},{32,160},{40,168},{48,176},{56,1... | collective-permute-start | bytes 786440 | tf_op jit(solution)/shard_map/ppermute | solution.py:14
  150.0 0.4 convolution_add_fusion.3
  150.4 3.2 %collective-permute-start.8 = (f32[4,128,128]{2,1,0:T(8,128)S(1)}, f32[4,128,128]{2,1,0:T(8,128)S(1)}, u32[]{:S(2)}, u32[]{:S(2)}) collective-permute-start(f32[4,128,128]{2,1,0:T(8,128)S(1)} %convolution_add_fusion.3), channel_id=1, source_target_pairs={{0,128},{8,136},{16,144},{24,152},{32,160},{40,168},{48,176},{56,1... | collective-permute-start | bytes 786440 | tf_op jit(solution)/shard_map/ppermute | solution.py:14
  154.4 0.4 fusion.32
  154.8 2.6 %collective-permute-done.9 = f32[4,128,128]{2,1,0:T(8,128)S(1)} collective-permute-done((f32[4,128,128]{2,1,0:T(8,128)S(1)}, f32[4,128,128]{2,1,0:T(8,128)S(1)}, u32[]{:S(2)}, u32[]{:S(2)}) %collective-permute-start.9) | collective-permute-done | bytes 262176 | tf_op jit(solution)/shard_map/ppermute | solution.py:14
  157.5 13.5 %collective-permute-done.8 = f32[4,128,128]{2,1,0:T(8,128)S(1)} collective-permute-done((f32[4,128,128]{2,1,0:T(8,128)S(1)}, f32[4,128,128]{2,1,0:T(8,128)S(1)}, u32[]{:S(2)}, u32[]{:S(2)}) %collective-permute-start.8) | collective-permute-done | bytes 262176 | tf_op jit(solution)/shard_map/ppermute | solution.py:14
  171.0 0.4 convolution_add_fusion.2
  171.4 11.8 %collective-permute-start.10 = (f32[4,128,128]{2,1,0:T(8,128)S(1)}, f32[4,128,128]{2,1,0:T(8,128)S(1)}, u32[]{:S(2)}, u32[]{:S(2)}) collective-permute-start(f32[4,128,128]{2,1,0:T(8,128)S(1)} %convolution_add_fusion.2), channel_id=1, source_target_pairs={{0,256},{8,264},{16,272},{24,280},{32,288},{40,296},{48,304},{56,3... | collective-permute-start | bytes 786440 | tf_op jit(solution)/shard_map/ppermute | solution.py:14
  183.1 0.4 convolution_select_fusion
  183.9 0.4 fusion.29
  184.4 6.0 %collective-permute-done.10 = f32[4,128,128]{2,1,0:T(8,128)S(1)} collective-permute-done((f32[4,128,128]{2,1,0:T(8,128)S(1)}, f32[4,128,128]{2,1,0:T(8,128)S(1)}, u32[]{:S(2)}, u32[]{:S(2)}) %collective-permute-start.10) | collective-permute-done | bytes 262176 | tf_op jit(solution)/shard_map/ppermute | solution.py:14
  191.3 4.6 %convolution_convert_fusion = bf16[128,4096]{1,0:T(8,128)(2,1)} fusion(bf16[512,4096]{0,1:T(8,128)(2,1)} %all-gather.2.cloned.1.call-done, bf16[16,8,4,128]{3,2,1,0:T(4,128)(2,1)S(1)} %bitcast.271), kind=kOutput, calls=%fused_computation.27 | convolution fusion | flops 537395200 | bytes 5373952 | tf_op jit(solution)/shard_map/dot_general | solution.py:152
  196.0 42.4 %reduce-scatter.2.cloned.1.call-done = bf16[128,512]{1,0:T(8,128)(2,1)} async-done(((bf16[128,4096]{1,0:T(8,128)(2,1)}), bf16[128,512]{1,0:T(8,128)(2,1)}) %reduce-scatter.2.cloned.1.call-update) | async-done | bytes 131088 | tf_op jit(solution)/shard_map/reduce_scatter | solution.py:157
  (66 shorter events, 9.3 us)
Async XLA Ops:
  6.5 184.8 %all-gather.2.cloned.1.call-start = ((), (), s32[]{:S(2)}) async-start(), calls=%async_computation.1 | async-start | bytes 4259840 | tf_op jit(solution)/shard_map/all_gather | solution.py:154
  7.3 231.1 %reduce-scatter.2.cloned.1.call-start = ((), (), s32[]{:S(2)}) async-start(), calls=%async_computation.2 | async-start | bytes 1179648 | tf_op jit(solution)/shard_map/reduce_scatter | solution.py:157
  58.0 9.2 %copy-start = (f32[128,4,7]{0,1,2:T(4,128)S(1)}, f32[128,4,7]{0,1,2:T(4,128)}, u32[]{:S(2)}) copy-start(f32[128,4,7]{0,1,2:T(4,128)} %param.14) | copy-start | bytes 43012
  61.3 7.8 %collective-permute-start.1 = (f32[4,128,128]{2,1,0:T(8,128)S(1)}, f32[4,128,128]{2,1,0:T(8,128)S(1)}, u32[]{:S(2)}, u32[]{:S(2)}) collective-permute-start(f32[4,128,128]{2,1,0:T(8,128)S(1)} %get-tuple-element.58), channel_id=1, source_target_pairs={{0,8},{8,0},{16,24},{24,16},{32,40},{40,32},{48,56},{56,48},{64,72... | collective-permute-start | bytes 786440 | tf_op jit(solution)/shard_map/ppermute | solution.py:14
  65.3 10.5 %collective-permute-start = (f32[4,128,128]{2,1,0:T(8,128)S(1)}, f32[4,128,128]{2,1,0:T(8,128)S(1)}, u32[]{:S(2)}, u32[]{:S(2)}) collective-permute-start(f32[4,128,128]{2,1,0:T(8,128)S(1)} %get-tuple-element.57), channel_id=1, source_target_pairs={{0,8},{8,0},{16,24},{24,16},{32,40},{40,32},{48,56},{56,48},{64,72... | collective-permute-start | bytes 786440 | tf_op jit(solution)/shard_map/ppermute | solution.py:14
  69.5 17.8 %collective-permute-start.3 = (f32[4,128,128]{2,1,0:T(8,128)S(1)}, f32[4,128,128]{2,1,0:T(8,128)S(1)}, u32[]{:S(2)}, u32[]{:S(2)}) collective-permute-start(f32[4,128,128]{2,1,0:T(8,128)S(1)} %fusion.70), channel_id=1, source_target_pairs={{0,16},{8,24},{16,0},{24,8},{32,48},{40,56},{48,32},{56,40},{64,80... | collective-permute-start | bytes 786440 | tf_op jit(solution)/shard_map/ppermute | solution.py:14
  76.2 33.5 %collective-permute-start.2 = (f32[4,128,128]{2,1,0:T(8,128)S(1)}, f32[4,128,128]{2,1,0:T(8,128)S(1)}, u32[]{:S(2)}, u32[]{:S(2)}) collective-permute-start(f32[4,128,128]{2,1,0:T(8,128)S(1)} %convolution_add_fusion.6), channel_id=1, source_target_pairs={{0,16},{8,24},{16,0},{24,8},{32,48},{40,56},{48,32},{56,40},{64,80... | collective-permute-start | bytes 786440 | tf_op jit(solution)/shard_map/ppermute | solution.py:14
  87.7 37.3 %collective-permute-start.5 = (f32[4,128,128]{2,1,0:T(8,128)S(1)}, f32[4,128,128]{2,1,0:T(8,128)S(1)}, u32[]{:S(2)}, u32[]{:S(2)}) collective-permute-start(f32[4,128,128]{2,1,0:T(8,128)S(1)} %fusion.67), channel_id=1, source_target_pairs={{0,32},{8,40},{16,48},{24,56},{32,0},{40,8},{48,16},{56,24},{64,96... | collective-permute-start | bytes 786440 | tf_op jit(solution)/shard_map/ppermute | solution.py:14
  110.2 24.2 %collective-permute-start.4 = (f32[4,128,128]{2,1,0:T(8,128)S(1)}, f32[4,128,128]{2,1,0:T(8,128)S(1)}, u32[]{:S(2)}, u32[]{:S(2)}) collective-permute-start(f32[4,128,128]{2,1,0:T(8,128)S(1)} %convolution_add_fusion.5), channel_id=1, source_target_pairs={{0,32},{8,40},{16,48},{24,56},{32,0},{40,8},{48,16},{56,24},{64,96... | collective-permute-start | bytes 786440 | tf_op jit(solution)/shard_map/ppermute | solution.py:14
  125.4 19.4 %collective-permute-start.7 = (f32[4,128,128]{2,1,0:T(8,128)S(1)}, f32[4,128,128]{2,1,0:T(8,128)S(1)}, u32[]{:S(2)}, u32[]{:S(2)}) collective-permute-start(f32[4,128,128]{2,1,0:T(8,128)S(1)} %fusion.64), channel_id=1, source_target_pairs={{0,64},{8,72},{16,80},{24,88},{32,96},{40,104},{48,112},{56,120},{... | collective-permute-start | bytes 786440 | tf_op jit(solution)/shard_map/ppermute | solution.py:14
  134.8 15.2 %collective-permute-start.6 = (f32[4,128,128]{2,1,0:T(8,128)S(1)}, f32[4,128,128]{2,1,0:T(8,128)S(1)}, u32[]{:S(2)}, u32[]{:S(2)}) collective-permute-start(f32[4,128,128]{2,1,0:T(8,128)S(1)} %convolution_add_fusion.4), channel_id=1, source_target_pairs={{0,64},{8,72},{16,80},{24,88},{32,96},{40,104},{48,112},{56,120},{... | collective-permute-start | bytes 786440 | tf_op jit(solution)/shard_map/ppermute | solution.py:14
  145.2 12.2 %collective-permute-start.9 = (f32[4,128,128]{2,1,0:T(8,128)S(1)}, f32[4,128,128]{2,1,0:T(8,128)S(1)}, u32[]{:S(2)}, u32[]{:S(2)}) collective-permute-start(f32[4,128,128]{2,1,0:T(8,128)S(1)} %fusion.61), channel_id=1, source_target_pairs={{0,128},{8,136},{16,144},{24,152},{32,160},{40,168},{48,176},{56,1... | collective-permute-start | bytes 786440 | tf_op jit(solution)/shard_map/ppermute | solution.py:14
  150.4 20.6 %collective-permute-start.8 = (f32[4,128,128]{2,1,0:T(8,128)S(1)}, f32[4,128,128]{2,1,0:T(8,128)S(1)}, u32[]{:S(2)}, u32[]{:S(2)}) collective-permute-start(f32[4,128,128]{2,1,0:T(8,128)S(1)} %convolution_add_fusion.3), channel_id=1, source_target_pairs={{0,128},{8,136},{16,144},{24,152},{32,160},{40,168},{48,176},{56,1... | collective-permute-start | bytes 786440 | tf_op jit(solution)/shard_map/ppermute | solution.py:14
  171.4 19.0 %collective-permute-start.10 = (f32[4,128,128]{2,1,0:T(8,128)S(1)}, f32[4,128,128]{2,1,0:T(8,128)S(1)}, u32[]{:S(2)}, u32[]{:S(2)}) collective-permute-start(f32[4,128,128]{2,1,0:T(8,128)S(1)} %convolution_add_fusion.2), channel_id=1, source_target_pairs={{0,256},{8,264},{16,272},{24,280},{32,288},{40,296},{48,304},{56,3... | collective-permute-start | bytes 786440 | tf_op jit(solution)/shard_map/ppermute | solution.py:14
Sparse Core Ops, SparseCore 0:
  10.4 119.4 all-gather.1
  196.1 42.2 reduce-scatter.1
where the time goes:
time: 247 us; the launch traced here: 245 us
  starting transfers between devices  83.3 us (34%)
  waiting for transfers between devices  78.7 us (32%)
  other arithmetic  40.4 us (16%)
  matrix products  23.3 us (9%)
  between operations  14.1 us (6%)
  local copies, waits for them, and re-layouts  5.21 us (2%)
    ppermute x11, starting transfers between devices, partner(): lax.ppermute(value, axis, [(i, i ^ 1 << apart) for i in range(lax.axis_si...  83.3 us
    reduce_scatter x1, waiting for transfers between devices, per_device(): lax.psum_scatter(partial_value.astype(jnp.float32).astype(jnp.bfloat16),...  42.4 us
    another operation x3, other arithmetic, span_terms(): jax.scipy.linalg.solve_triangular(system, right_side, lower=True, unit_di...  39.4 us
    ppermute x11, waiting for transfers between devices, partner(): lax.ppermute(value, axis, [(i, i ^ 1 << apart) for i in range(lax.axis_si...  35.6 us
  transfers between devices with their start and end apart: 13, of which 6 were waited for; matrix products, arithmetic and copies ran while one was open for 26% of the time, Pallas kernels for 0%

commit v1 on v0

v1 whole, which is shorter than its diff:
```python
import jax
import jax.numpy as jnp
from jax import lax
from jax.sharding import PartitionSpec as P
from jax.experimental import pallas as pl
from jax.experimental.pallas import tpu as pltpu

DK = 128
TB = 128
MESH = pl.DeviceIdType.MESH
F32 = jnp.float32
BF16 = jnp.bfloat16


def split(a):
    hi = a.astype(BF16)
    lo = (a - hi.astype(F32)).astype(BF16)
    return hi, lo


def dot3(a, b):
    ah, al = split(a)
    bh, bl = split(b)
    return jnp.dot(
        jnp.concatenate([ah, ah, al], axis=1),
        jnp.concatenate([bh, bl, bh], axis=0),
        preferred_element_type=F32,
    )


def dot3_nt(a, b):
    ah, al = split(a)
    bh, bl = split(b)
    return lax.dot_general(
        jnp.concatenate([ah, ah, al], axis=1),
        jnp.concatenate([bh, bl, bh], axis=1),
        (((1,), (1,)), ((), ())),
        preferred_element_type=F32,
    )


def unit_rows(x):
    return x * lax.rsqrt(jnp.sum(x * x, axis=-1, keepdims=True) + 1e-06)


def kernel(
    q_ref, k_ref, v_ref, dec_ref, beta_ref, lw_ref, w_ref, out_ref,
    small, rq, rk, rv, rs, kn, gm, wu, ab, cols, lrt, ot, tot, relay,
    st_send, st_recv, osend, mt, wg, acc, sib_send, sib_recv, x_send, x_recv,
    kv_ss, kv_rs, q_ss, q_rs, st_ss, st_rs, o_ss, o_rs, w1_ss, w1_rs, w2_ss, w2_rs,
    sb_ss, sb_rs, x_ss, x_rs,
):
    ctx = lax.axis_index("ctx")
    head = lax.axis_index("head")
    zi = ctx // 8
    yi = ctx % 8
    yl = ctx % 4
    base = ctx - yl
    core = head % 2
    xi = head // 2

    def at_zy(z, y):
        return {"ctx": z * 8 + y}

    barrier = pltpu.get_barrier_semaphore()
    for d in range(1, 8):
        pl.semaphore_signal(barrier, inc=1, device_id=at_zy(zi, (yi + d) % 8), device_id_type=MESH)
        pl.semaphore_signal(barrier, inc=1, device_id=at_zy((zi + d) % 8, yi), device_id_type=MESH)
    for d in range(1, 4):
        pl.semaphore_signal(
            barrier, inc=1, device_id={"head": ((xi + d) % 4) * 2 + core}, device_id_type=MESH
        )
    pl.semaphore_signal(barrier, inc=1, device_id={"head": head ^ 1}, device_id_type=MESH)

    pack = jnp.concatenate(
        [dec_ref[...], beta_ref[...], lw_ref[...], jnp.zeros((TB, 92), F32)], axis=1
    ).T
    for j in range(4):
        small[j, 0:1, :] = pack[j : j + 1]
        small[j, 1:2, :] = pack[4 + j : 5 + j]
        small[j, 2:9, :] = pack[8 + 7 * j : 15 + 7 * j]
        small[j, 9:16, :] = jnp.zeros((7, TB), F32)
    wg[zi, yi] = w_ref[...].astype(F32).T.astype(BF16)

    pl.semaphore_wait(barrier, 18)

    def lane(j):
        return pl.ds(pl.multiple_of(j * DK, DK), DK)

    kv_copies = []
    for d in (3, 2, 1):
        to = (yl + d) % 4
        for a, (src, dst) in enumerate(
            ((k_ref.at[:, lane(to)], rk), (v_ref.at[:, lane(to)], rv), (small.at[to], rs))
        ):
            cp = pltpu.make_async_remote_copy(
                src_ref=src, dst_ref=dst.at[yl], send_sem=kv_ss.at[a, d], recv_sem=kv_rs.at[a, d],
                device_id={"ctx": base + to}, device_id_type=MESH,
            )
            cp.start()
            kv_copies.append(cp)

    def w1_copy(half, d):
        to = at_zy((zi + d) % 8, yi) if half == 0 else at_zy(zi, (yi + d) % 8)
        part = wg.at[zi, yi, pl.ds(32 * half, 32)]
        return pltpu.make_async_remote_copy(
            src_ref=part, dst_ref=part, send_sem=w1_ss.at[half, d], recv_sem=w1_rs.at[half, d],
            device_id=to, device_id_type=MESH,
        )

    w1 = [[w1_copy(half, d) for d in range(1, 8)] for half in range(2)]
    for cp in w1[0]:
        cp.start()

    def w2_copy(half, way, step):
        mine = yi if half == 0 else zi
        slot = (mine + (-(step - 1) if way == 0 else step - 1) + 8) % 8
        nxt = (mine + (1 if way == 0 else 7)) % 8
        to = at_zy(zi, nxt) if half == 0 else at_zy(nxt, yi)
        low = 32 * half
        size = 32
        if step == 4:
            low = low + 16 * way
            size = 16
        part = wg.at[:, slot, pl.ds(low, size)] if half == 0 else wg.at[slot, :, pl.ds(low, size)]
        return pltpu.make_async_remote_copy(
            src_ref=part, dst_ref=part,
            send_sem=w2_ss.at[half, way, step], recv_sem=w2_rs.at[half, way, step],
            device_id=to, device_id_type=MESH,
        )

    w2 = [[[w2_copy(h, w, s) for s in range(1, 5)] for w in range(2)] for h in range(2)]

    def w2_start(half, step):
        for way in range(2):
            w2[half][way][step - 1].start()

    def w2_wait(half, step):
        for way in range(2):
            w2[half][way][step - 1].wait_recv()

    rq[yl] = q_ref[:, lane(yl)]
    rk[yl] = k_ref[:, lane(yl)]
    rv[yl] = v_ref[:, lane(yl)]
    rs[yl] = small[yl]

    ri = lax.broadcasted_iota(jnp.int32, (TB, TB), 0)
    ci = lax.broadcasted_iota(jnp.int32, (TB, TB), 1)
    eye = (ri == ci).astype(F32)
    upto = (ri <= ci).astype(F32)

    def pairs(slots):
        n = len(slots)
        ls, rhs, keys, tails, lasts = [], [], [], [], []
        for s in slots:
            sm = rs[s]
            g_rows = -jnp.dot(
                sm, upto, preferred_element_type=F32, precision=lax.Precision.HIGHEST
            )
            g_row = g_rows[0:1]
            col = jnp.concatenate([g_row, sm[1:8]], axis=0)
            col = jnp.concatenate([col, jnp.zeros((TB - 8, TB), F32)], axis=0).T
            g_col = col[:, 0:1]
            b_col = col[:, 1:2]
            growth = jnp.exp(g_col)
            g_last = g_row[:, TB - 1 : TB]
            ratio = jnp.where(ci <= ri, jnp.exp(jnp.minimum(g_col - g_row, 0.0)), 0.0)
            kk = unit_rows(rk[s].astype(F32))
            kn[s] = kk
            gm[s] = ratio
            cols[s] = jnp.broadcast_to(growth, (TB, DK))
            ls.append(jnp.where(ci < ri, b_col * ratio * dot3_nt(kk, kk), 0.0))
            rhs.append(
                jnp.concatenate([(b_col * growth) * kk, b_col * rv[s].astype(F32)], axis=1)
            )
            tails.append(jnp.exp(g_last - g_col) * kk)
            lasts.append(jnp.exp(g_last))
        inv = [eye - jnp.where((ri % 2 == 1) & (ci == ri - 1), l, 0.0) for l in ls]
        b = 2
        while b < TB:
            mask = ((ri // b) % 2 == 1) & (ci // b == ri // b - 1)
            mid = [dot3(inv[i], jnp.where(mask, ls[i], 0.0)) for i in range(n)]
            inv = [inv[i] - dot3(mid[i], inv[i]) for i in range(n)]
            b *= 2
        sol = [dot3(inv[i], rhs[i]) for i in range(n)]
        for i, s in enumerate(slots):
            wu[s] = sol[i]
            m = dot3(tails[i].T, sol[i])
            ab[s, :, 0:DK] = lasts[i] * eye - m[:, 0:DK]
            ab[s, :, DK:] = m[:, DK:]

    pairs([yl])

    for cp in kv_copies:
        cp.wait_recv()
    q_copies = []
    for d in (3, 2, 1):
        to = (yl + d) % 4
        cp = pltpu.make_async_remote_copy(
            src_ref=q_ref.at[:, lane(to)], dst_ref=rq.at[yl], send_sem=q_ss.at[d], recv_sem=q_rs.at[d],
            device_id={"ctx": base + to}, device_id_type=MESH,
        )
        cp.start()
        q_copies.append(cp)
    for cp in w1[1]:
        cp.start()

    pairs([(yl + d) % 4 for d in range(1, 4)])

    def apply(second, first):
        r = dot3(second[:, 0:DK], first)
        return jnp.concatenate([r[:, 0:DK], r[:, DK:] + second[:, DK:]], axis=1)

    ab01 = apply(ab[1], ab[0])
    ab23 = apply(ab[3], ab[2])
    group = apply(ab23, ab01)

    def level_copy(i):
        if i < 3:
            src, dst = st_send.at[i], st_recv.at[i]
        else:
            src, dst = st_send.at[i, :, pl.ds(DK, DK)], st_recv.at[i, :, pl.ds(DK, DK)]
        return pltpu.make_async_remote_copy(
            src_ref=src, dst_ref=dst, send_sem=st_ss.at[i], recv_sem=st_rs.at[i],
            device_id={"ctx": ctx ^ (4 << i)}, device_id_type=MESH,
        )

    levels = [level_copy(i) for i in range(4)]
    tot[...] = group
    st_send[0] = group.astype(BF16)
    levels[0].start()
    relay[...] = eye

    for cp in w1[0]:
        cp.wait_recv()
    w2_start(0, 1)

    for cp in q_copies:
        cp.wait_recv()
    b01 = ab01[:, DK:]
    a2 = ab[2, :, 0:DK]
    r3 = dot3(a2, ab01)
    starts = [None, ab[0, :, 0:DK], ab01[:, 0:DK], r3[:, 0:DK]]
    for s in range(4):
        kk = kn[s]
        qq = unit_rows(rq[s].astype(F32))
        p = dot3_nt(qq, kk) * gm[s]
        pwu = dot3(p, wu[s])
        moved = cols[s] * qq - pwu[:, 0:DK]
        inner = pwu[:, DK:]
        wt = rs[s]
        o = wt[2:3] * inner.T
        if s == 0:
            lifted = moved
        elif s == 1:
            r = dot3(moved, ab[0])
            lifted = r[:, 0:DK]
            o = o + wt[3:4] * r[:, DK:].T
        elif s == 2:
            r = dot3(moved, ab01)
            lifted = r[:, 0:DK]
            o = o + wt[4:5] * r[:, DK:].T
        else:
            r = dot3(moved, jnp.concatenate([r3, ab[2, :, DK:]], axis=1))
            lifted = r[:, 0:DK]
            o = o + wt[4:5] * r[:, DK : 2 * DK].T + wt[3:4] * r[:, 2 * DK :].T
        lrt[:, s * TB : (s + 1) * TB] = lifted.T
        ot[:, s * TB : (s + 1) * TB] = o

    def add_level(i, state):
        t = dot3(state.T, lrt[...])
        for s in range(4):
            sl = slice(s * TB, (s + 1) * TB)
            ot[:, sl] = ot[:, sl] + rs[s, 4 + i + 1 : 4 + i + 2, :] * t[:, sl]

    for cp in w1[1]:
        cp.wait_recv()
    w2_start(1, 1)

    for i in range(4):
        upper = (ctx // (4 << i)) % 2 == 1
        if i < 3:
            levels[i].wait_recv()
            other = st_recv[i].astype(F32)
            own = tot[...]
            first = jnp.where(upper, other, own)
            second = jnp.where(upper, own, other)
            old = relay[...]
            r = dot3(jnp.concatenate([second[:, 0:DK], old], axis=0), first)
            new_b = r[0:DK, DK:] + second[:, DK:]
            tot[:, 0:DK] = r[0:DK, 0:DK]
            tot[:, DK:] = new_b
            st_send[i + 1, :, 0:DK] = r[0:DK, 0:DK].astype(BF16)
            st_send[i + 1, :, DK:] = new_b.astype(BF16)
            if i < 2:
                levels[i + 1].start()
            else:
                @pl.when((ctx // 32) % 2 == 0)
                def _():
                    levels[3].start()
            relay[...] = jnp.where(upper, r[DK:, 0:DK], old)

            @pl.when(upper)
            def _():
                add_level(i, r[DK:, DK:])

            w2_wait(0, i + 1)
            w2_start(0, i + 2)
            w2_wait(1, i + 1)
            w2_start(1, i + 2)
        else:
            @pl.when(upper)
            def _():
                levels[3].wait_recv()
                add_level(3, dot3(relay[...], st_recv[3, :, DK:].astype(F32)))

            @pl.when(jnp.logical_not(upper))
            def _():
                levels[3].wait_send()

    osend[...] = ot[...].astype(BF16)
    o_copies = []
    for d in (3, 2, 1):
        to = (yl + d) % 4
        cp = pltpu.make_async_remote_copy(
            src_ref=osend.at[:, lane(to)], dst_ref=mt.at[pl.ds(pl.multiple_of(yl * DK, DK), DK)],
            send_sem=o_ss.at[d], recv_sem=o_rs.at[d],
            device_id={"ctx": base + to}, device_id_type=MESH,
        )
        cp.start()
        o_copies.append(cp)
    mt[pl.ds(pl.multiple_of(yl * DK, DK), DK)] = osend[:, lane(yl)]
    w2_wait(0, 4)
    w2_wait(1, 4)
    for cp in o_copies:
        cp.wait_recv()

    def share(block):
        w = wg[block].reshape(512, 512)
        return jnp.dot(w, mt[...], preferred_element_type=F32)

    order = (2, 1, 3, 0)
    sib = []
    for j, d in enumerate(order):
        sib_send[j] = share(((xi + d) % 4) * 2 + 1 - core).astype(BF16)
        cp = pltpu.make_async_remote_copy(
            src_ref=sib_send.at[j], dst_ref=sib_recv.at[j], send_sem=sb_ss.at[j], recv_sem=sb_rs.at[j],
            device_id={"head": head ^ 1}, device_id_type=MESH,
        )
        cp.start()
        sib.append(cp)
    xs = []
    for j, d in enumerate(order):
        acc[...] = share(((xi + d) % 4) * 2 + core)
        sib[j].wait_recv()
        total = acc[...] + sib_recv[j].astype(F32)
        if d != 0:
            x_send[d] = total.astype(BF16)
            cp = pltpu.make_async_remote_copy(
                src_ref=x_send.at[d], dst_ref=x_recv.at[d], send_sem=x_ss.at[d], recv_sem=x_rs.at[d],
                device_id={"head": ((xi + d) % 4) * 2 + core}, device_id_type=MESH,
            )
            cp.start()
            xs.append((d, cp))
    for d, cp in xs:
        cp.wait_recv()
        total = total + x_recv[d].astype(F32)
    out_ref[...] = total.T.astype(BF16)

    for cp in kv_copies + q_copies + levels[:3] + o_copies + sib + [c for _, c in xs]:
        cp.wait_send()
    for half in range(2):
        for cp in w1[half]:
            cp.wait_send()
        for way in range(2):
            for cp in w2[half][way]:
                cp.wait_send()


def per_device(q, k, v, dec, beta, lw, w):
    vmem = pl.BlockSpec(memory_space=pltpu.VMEM)
    dma = pltpu.SemaphoreType.DMA
    return pl.pallas_call(
        kernel,
        out_shape=jax.ShapeDtypeStruct((TB, 512), BF16),
        in_specs=[vmem] * 7,
        out_specs=vmem,
        scratch_shapes=[
            pltpu.VMEM((4, 16, TB), F32),
            pltpu.VMEM((4, TB, DK), BF16),
            pltpu.VMEM((4, TB, DK), BF16),
            pltpu.VMEM((4, TB, DK), BF16),
            pltpu.VMEM((4, 16, TB), F32),
            pltpu.VMEM((4, TB, DK), F32),
            pltpu.VMEM((4, TB, TB), F32),
            pltpu.VMEM((4, TB, 2 * DK), F32),
            pltpu.VMEM((4, DK, 2 * DK), F32),
            pltpu.VMEM((4, TB, DK), F32),
            pltpu.VMEM((DK, 4 * TB), F32),
            pltpu.VMEM((DK, 4 * TB), F32),
            pltpu.VMEM((DK, 2 * DK), F32),
            pltpu.VMEM((DK, DK), F32),
            pltpu.VMEM((4, DK, 2 * DK), BF16),
            pltpu.VMEM((4, DK, 2 * DK), BF16),
            pltpu.VMEM((DK, 4 * TB), BF16),
            pltpu.VMEM((4 * DK, TB), BF16),
            pltpu.VMEM((8, 8, 64, 512), BF16),
            pltpu.VMEM((512, TB), F32),
            pltpu.VMEM((4, 512, TB), BF16),
            pltpu.VMEM((4, 512, TB), BF16),
            pltpu.VMEM((4, 512, TB), BF16),
            pltpu.VMEM((4, 512, TB), BF16),
            dma((3, 4)), dma((3, 4)), dma((4,)), dma((4,)), dma((4,)), dma((4,)),
            dma((4,)), dma((4,)), dma((2, 8)), dma((2, 8)), dma((2, 2, 5)), dma((2, 2, 5)),
            dma((4,)), dma((4,)), dma((4,)), dma((4,)),
        ],
        compiler_params=pltpu.CompilerParams(
            collective_id=0, has_side_effects=True, vmem_limit_bytes=40 * 2**20
        ),
        name="mixer",
    )(q, k, v, dec, beta, lw.reshape(TB, 28), w)


def solution(mesh):
    spec = P("ctx", "head")
    return jax.shard_map(
        per_device,
        mesh=mesh,
        in_specs=(spec,) * 5 + (P("ctx", "head", None), P("head", "ctx")),
        out_specs=spec,
        check_vma=False,
    )
```

time: 247 us -> 81.3 us (0.33)
  starting transfers between devices: 83.3 us -> 0 us
  waiting for transfers between devices: 78.7 us -> 0 us
  Pallas kernels: 0 us -> 77.3 us
  other arithmetic: 40.4 us -> 0 us
  matrix products: 23.3 us -> 0 us
  between operations: 14.1 us -> 0.03 us
    ppermute x11 -> x0, starting transfers between devices: 83.3 us -> none  [partner(): lax.ppermute(value, axis, [(i, i ^ 1 << apart) for i in range(lax.axis_si...]
    pallas_call x0 -> x1, Pallas kernels: none -> 77.3 us  [per_device(): pl.pallas_call(kernel, out_shape=jax.ShapeDtypeStruct((TB, 512), BF16), i...]
    reduce_scatter x1 -> x0, waiting for transfers between devices: 42.4 us -> none  [per_device(): lax.psum_scatter(partial_value.astype(jnp.float32).astype(jnp.bfloat16),...]
    another operation x5 -> x0, other arithmetic: 39.4 us -> none  [the longest x3 39.4 us: span_terms(): jax.scipy.linalg.solve_triangular(system, right_side, lower=True, unit_di...]
    ppermute x11 -> x0, waiting for transfers between devices: 35.6 us -> none  [partner(): lax.ppermute(value, axis, [(i, i ^ 1 << apart) for i in range(lax.axis_si...]
    dot_general x42 -> x0, matrix products: 22.7 us -> none  [the longest x1 4.62 us: per_device(): jnp.dot(mixer_out, lax.all_gather(out_weight, 'ctx', axis=1, tiled=True),...]
    unnamed x3 -> x17, local copies, waits for them, and re-layouts: 0.09 us -> 3.6 us
    reshape x5 -> x2, local copies, waits for them, and re-layouts: 2.62 us -> 0.11 us  [per_device(): lw.reshape(TB, 28)]
  transfers between devices with their start and end apart: 13 -> 0, of which waited for: 6 -> 0; matrix products, arithmetic and copies ran while one was open for 26% -> 0% of each run, Pallas kernels for 0% -> 0%
where the time goes in v1:
time: 81.3 us; the launch traced here: 81 us
  Pallas kernels  77.3 us (95%)
  local copies, waits for them, and re-layouts  3.71 us (5%)
    pallas_call x1, Pallas kernels, per_device(): pl.pallas_call(kernel, out_shape=jax.ShapeDtypeStruct((TB, 512), BF16), i...  77.3 us
    unnamed x17, local copies, waits for them, and re-layouts  3.6 us

profile of v1, /device:TPU:1, one launch (start us, length us, event | category | flops | bytes accessed | tf_op | source)
XLA Modules:
  0.0 81.0 jit_solution(16890867368261640001)
XLA Ops:
  0.0 0.0 copy-start.3
  0.0 0.7 copy.12
  0.7 0.0 copy-start.4
  0.8 0.0 copy-start.2
  0.8 0.1 copy.15.lw_ref
  0.9 0.6 copy-done.4
  1.4 0.0 copy-start.5
  1.4 0.1 copy.13.dec_ref
  1.5 0.6 copy-done.5
  2.1 0.0 copy-start
  2.1 0.0 copy-start.1
  2.1 0.1 copy.14.beta_ref
  2.2 0.0 copy-done.3
  2.2 0.1 copy.16.w_ref
  2.4 0.0 copy-done.2
  2.4 0.7 copy-done
  3.0 0.1 copy-done.1
  3.1 77.3 %mixer.1 = bf16[128,512]{1,0:T(8,128)(2,1)S(1)} custom-call(bf16[128,512]{1,0:T(8,128)(2,1)S(1)} %copy-done, bf16[128,512]{1,0:T(8,128)(2,1)S(1)} %copy-done.1, bf16[128,512]{1,0:T(8,128)(2,1)S(1)} %copy-done.2, f32[128,4]{1,0:T(8,128)S(1)} %copy.13.dec_ref, f32[128,4]{1,0:T(8,128)S(1)} %copy.14.beta_ref, f32[128,28]{1,0:T(8,128)S(1)} %copy.15.lw_ref, ...), custom_call_target="tpu_custom_call" | custom-call | tf_op jit(solution)/shard_map/mixer/pallas_call | solution.py:383
  80.4 0.7 copy.18
  (1 shorter events, 0.0 us)
Async XLA Ops:
  0.0 2.2 %copy-start.3 = (bf16[512,64]{0,1:T(8,128)(2,1)S(1)}, bf16[512,64]{0,1:T(8,128)(2,1)}, u32[]{:S(2)}) copy-start(bf16[512,64]{0,1:T(8,128)(2,1)} %param.13) | copy-start | bytes 196612
  0.7 0.7 copy-start.4
  0.8 1.6 %copy-start.2 = (bf16[128,512]{1,0:T(8,128)(2,1)S(1)}, bf16[128,512]{1,0:T(8,128)(2,1)}, u32[]{:S(2)}) copy-start(bf16[128,512]{1,0:T(8,128)(2,1)} %v_ref.1) | copy-start | bytes 393220
  1.4 0.7 copy-start.5
  2.1 0.9 %copy-start = (bf16[128,512]{1,0:T(8,128)(2,1)S(1)}, bf16[128,512]{1,0:T(8,128)(2,1)}, u32[]{:S(2)}) copy-start(bf16[128,512]{1,0:T(8,128)(2,1)} %q_ref.1) | copy-start | bytes 393220
  2.1 1.0 %copy-start.1 = (bf16[128,512]{1,0:T(8,128)(2,1)S(1)}, bf16[128,512]{1,0:T(8,128)(2,1)}, u32[]{:S(2)}) copy-start(bf16[128,512]{1,0:T(8,128)(2,1)} %k_ref.1) | copy-start | bytes 393220

commit v2 on v1

v2 whole, which is shorter than its diff:
```python
import jax
import jax.numpy as jnp
from jax import lax
from jax.sharding import PartitionSpec as P
from jax.experimental import pallas as pl
from jax.experimental.pallas import tpu as pltpu

DK = 128
TB = 128
MESH = pl.DeviceIdType.MESH
F32 = jnp.float32
BF16 = jnp.bfloat16


def split(a):
    hi = a.astype(BF16)
    lo = (a - hi.astype(F32)).astype(BF16)
    return hi, lo


def dot3(a, b):
    ah, al = split(a)
    bh, bl = split(b)
    return jnp.dot(
        jnp.concatenate([ah, ah, al], axis=1),
        jnp.concatenate([bh, bl, bh], axis=0),
        preferred_element_type=F32,
    )


def dot3_nt(a, b):
    ah, al = split(a)
    bh, bl = split(b)
    return lax.dot_general(
        jnp.concatenate([ah, ah, al], axis=1),
        jnp.concatenate([bh, bl, bh], axis=1),
        (((1,), (1,)), ((), ())),
        preferred_element_type=F32,
    )


def unit_rows(x):
    return x * lax.rsqrt(jnp.sum(x * x, axis=-1, keepdims=True) + 1e-06)


class Copies:
    def __init__(self):
        self.sends = []
        self.arrivals = []

    def start(self, *copies):
        for cp in copies:
            cp.start()
            self.sends.append(cp)
            self.arrivals.append(cp)

    def arrive(self, *copies):
        for cp in copies:
            cp.wait_recv()
            self.arrivals = [c for c in self.arrivals if c is not cp]

    def finish(self):
        for cp in self.arrivals:
            cp.wait_recv()
        for cp in self.sends:
            cp.wait_send()


def kernel(
    q_ref, k_ref, v_ref, dec_hbm, beta_hbm, lw_hbm, w_ref, out_ref,
    dec_ref, beta_ref, lw_ref, small, rq, rk, rv, rs, kn, gm, wu, ab, cols, lrt, ot, tot, relay,
    st_send, st_recv, mt, wg, sib_send, sib_recv, x_send, x_recv, fsend, fin,
    kv_ss, kv_rs, q_ss, q_rs, st_ss, st_rs, o_ss, o_rs, w1_ss, w1_rs, w2_ss, w2_rs,
    sb_ss, sb_rs, x_ss, x_rs, f_ss, f_rs, in_s,
):
    net = Copies()
    ctx = lax.axis_index("ctx")
    head = lax.axis_index("head")
    zi = ctx // 8
    yi = ctx % 8
    yl = ctx % 4
    yh = yi // 4
    base = ctx - yl
    core = head % 2
    xi = head // 2

    def at_zy(z, y):
        return {"ctx": z * 8 + y}

    def lane(j):
        return pl.ds(pl.multiple_of(j * DK, DK), DK)

    loads = [
        pltpu.make_async_copy(src, dst, in_s.at[i])
        for i, (src, dst) in enumerate(
            (
                (dec_hbm, dec_ref), (beta_hbm, beta_ref), (lw_hbm, lw_ref),
                (w_ref, wg.at[zi, yh]), (k_ref.at[:, lane(yl)], rk.at[yl]),
                (v_ref.at[:, lane(yl)], rv.at[yl]), (q_ref.at[:, lane(yl)], rq.at[yl]),
            )
        )
    ]
    for cp in loads:
        cp.start()

    barrier = pltpu.get_barrier_semaphore()
    for d in range(1, 8):
        pl.semaphore_signal(barrier, inc=1, device_id=at_zy((zi + d) % 8, yi), device_id_type=MESH)
    pl.semaphore_signal(barrier, inc=1, device_id={"ctx": ctx ^ 4}, device_id_type=MESH)
    for d in range(1, 4):
        pl.semaphore_signal(
            barrier, inc=1, device_id={"ctx": base + (yl + d) % 4}, device_id_type=MESH
        )
    for d in range(1, 4):
        pl.semaphore_signal(
            barrier, inc=1, device_id={"head": ((xi + d) % 4) * 2 + core}, device_id_type=MESH
        )
    pl.semaphore_signal(barrier, inc=1, device_id={"head": head ^ 1}, device_id_type=MESH)

    for cp in loads[:3]:
        cp.wait()
    for j in range(4):
        small[j, 0:1, :] = dec_ref[j : j + 1]
        small[j, 1:2, :] = beta_ref[j : j + 1]
        for l in range(7):
            small[j, 2 + l : 3 + l, :] = lw_ref[l, j : j + 1]
        small[j, 9:16, :] = jnp.zeros((7, TB), F32)

    pl.semaphore_wait(barrier, 15)

    kv_copies = []
    for d in (3, 2, 1):
        to = (yl + d) % 4
        for a, (src, dst) in enumerate(
            ((k_ref.at[:, lane(to)], rk), (v_ref.at[:, lane(to)], rv), (small.at[to], rs))
        ):
            cp = pltpu.make_async_remote_copy(
                src_ref=src, dst_ref=dst.at[yl], send_sem=kv_ss.at[a, d], recv_sem=kv_rs.at[a, d],
                device_id={"ctx": base + to}, device_id_type=MESH,
            )
            net.start(cp)
            kv_copies.append(cp)

    loads[3].wait()
    w_pair = pltpu.make_async_remote_copy(
        src_ref=wg.at[zi, yh], dst_ref=wg.at[zi, yh], send_sem=w1_ss, recv_sem=w1_rs,
        device_id={"ctx": ctx ^ 4}, device_id_type=MESH,
    )
    net.start(w_pair)

    def w_copy(way, step):
        slot = (zi + (step - 1) * (2 * way - 1) + 8) % 8
        part = wg.at[slot] if step < 4 else wg.at[slot, way]
        return pltpu.make_async_remote_copy(
            src_ref=part, dst_ref=part, send_sem=w2_ss.at[way, step], recv_sem=w2_rs.at[way, step],
            device_id=at_zy((zi + 1 + 6 * way) % 8, yi), device_id_type=MESH,
        )

    w_ring = [[w_copy(way, step) for way in range(2)] for step in range(1, 5)]

    def w_pass_on(step):
        net.arrive(*w_ring[step - 1])
        net.start(*w_ring[step])

    rs[yl] = small[yl]
    for cp in loads[4:]:
        cp.wait()

    ri = lax.broadcasted_iota(jnp.int32, (TB, TB), 0)
    ci = lax.broadcasted_iota(jnp.int32, (TB, TB), 1)
    eye = (ri == ci).astype(F32)
    upto = (ri <= ci).astype(F32)

    def pairs(slots):
        n = len(slots)
        ls, rhs, keys, tails, lasts = [], [], [], [], []
        for s in slots:
            sm = rs[s]
            g_rows = -jnp.dot(
                sm, upto, preferred_element_type=F32, precision=lax.Precision.HIGHEST
            )
            g_row = g_rows[0:1]
            col = jnp.concatenate([g_row, sm[1:8]], axis=0)
            col = jnp.concatenate([col, jnp.zeros((TB - 8, TB), F32)], axis=0).T
            g_col = col[:, 0:1]
            b_col = col[:, 1:2]
            growth = jnp.exp(g_col)
            g_last = g_row[:, TB - 1 : TB]
            ratio = jnp.where(ci <= ri, jnp.exp(jnp.minimum(g_col - g_row, 0.0)), 0.0)
            kk = unit_rows(rk[s].astype(F32))
            kn[s] = kk
            gm[s] = ratio
            cols[s] = jnp.broadcast_to(growth, (TB, DK))
            ls.append(jnp.where(ci < ri, b_col * ratio * dot3_nt(kk, kk), 0.0))
            rhs.append(
                jnp.concatenate([(b_col * growth) * kk, b_col * rv[s].astype(F32)], axis=1)
            )
            tails.append(jnp.exp(g_last - g_col) * kk)
            lasts.append(jnp.exp(g_last))
        inv = [eye - jnp.where((ri % 2 == 1) & (ci == ri - 1), l, 0.0) for l in ls]
        b = 2
        while b < TB:
            mask = ((ri // b) % 2 == 1) & (ci // b == ri // b - 1)
            mid = [dot3(inv[i], jnp.where(mask, ls[i], 0.0)) for i in range(n)]
            inv = [inv[i] - dot3(mid[i], inv[i]) for i in range(n)]
            b *= 2
        sol = [dot3(inv[i], rhs[i]) for i in range(n)]
        for i, s in enumerate(slots):
            wu[s] = sol[i]
            m = dot3(tails[i].T, sol[i])
            ab[s, :, 0:DK] = lasts[i] * eye - m[:, 0:DK]
            ab[s, :, DK:] = m[:, DK:]

    pairs([yl])
    net.arrive(w_pair)
    net.start(*w_ring[0])

    net.arrive(*kv_copies)
    q_copies = []
    for d in (3, 2, 1):
        to = (yl + d) % 4
        cp = pltpu.make_async_remote_copy(
            src_ref=q_ref.at[:, lane(to)], dst_ref=rq.at[yl], send_sem=q_ss.at[d], recv_sem=q_rs.at[d],
            device_id={"ctx": base + to}, device_id_type=MESH,
        )
        net.start(cp)
        q_copies.append(cp)
    w_pass_on(1)

    pairs([(yl + d) % 4 for d in range(1, 4)])

    def apply(second, first):
        r = dot3(second[:, 0:DK], first)
        return jnp.concatenate([r[:, 0:DK], r[:, DK:] + second[:, DK:]], axis=1)

    ab01 = apply(ab[1], ab[0])
    ab23 = apply(ab[3], ab[2])
    group = apply(ab23, ab01)

    def level_copy(i):
        if i < 3:
            src, dst = st_send.at[i], st_recv.at[i]
        else:
            src, dst = st_send.at[i, :, pl.ds(DK, DK)], st_recv.at[i, :, pl.ds(DK, DK)]
        return pltpu.make_async_remote_copy(
            src_ref=src, dst_ref=dst, send_sem=st_ss.at[i], recv_sem=st_rs.at[i],
            device_id={"ctx": ctx ^ (4 << i)}, device_id_type=MESH,
        )

    levels = [level_copy(i) for i in range(4)]
    tot[...] = group
    st_send[0] = group.astype(BF16)
    net.start(levels[0])
    relay[...] = eye

    net.arrive(*q_copies)
    b01 = ab01[:, DK:]
    a2 = ab[2, :, 0:DK]
    r3 = dot3(a2, ab01)
    starts = [None, ab[0, :, 0:DK], ab01[:, 0:DK], r3[:, 0:DK]]
    for s in range(4):
        kk = kn[s]
        qq = unit_rows(rq[s].astype(F32))
        p = dot3_nt(qq, kk) * gm[s]
        pwu = dot3(p, wu[s])
        moved = cols[s] * qq - pwu[:, 0:DK]
        inner = pwu[:, DK:]
        wt = rs[s]
        o = wt[2:3] * inner.T
        if s == 0:
            lifted = moved
        elif s == 1:
            r = dot3(moved, ab[0])
            lifted = r[:, 0:DK]
            o = o + wt[3:4] * r[:, DK:].T
        elif s == 2:
            r = dot3(moved, ab01)
            lifted = r[:, 0:DK]
            o = o + wt[4:5] * r[:, DK:].T
        else:
            r = dot3(moved, jnp.concatenate([r3, ab[2, :, DK:]], axis=1))
            lifted = r[:, 0:DK]
            o = o + wt[4:5] * r[:, DK : 2 * DK].T + wt[3:4] * r[:, 2 * DK :].T
        lrt[:, s * TB : (s + 1) * TB] = lifted.T
        ot[:, s * TB : (s + 1) * TB] = o

    def add_level(i, state):
        t = dot3(state.T, lrt[...])
        for s in range(4):
            sl = slice(s * TB, (s + 1) * TB)
            ot[:, sl] = ot[:, sl] + rs[s, 4 + i + 1 : 4 + i + 2, :] * t[:, sl]

    w_pass_on(2)

    for i in range(4):
        upper = (ctx // (4 << i)) % 2 == 1
        if i < 3:
            net.arrive(levels[i])
            other = st_recv[i].astype(F32)
            own = tot[...]
            first = jnp.where(upper, other, own)
            second = jnp.where(upper, own, other)
            old = relay[...]
            r = dot3(jnp.concatenate([second[:, 0:DK], old], axis=0), first)
            new_b = r[0:DK, DK:] + second[:, DK:]
            tot[:, 0:DK] = r[0:DK, 0:DK]
            tot[:, DK:] = new_b
            st_send[i + 1, :, 0:DK] = r[0:DK, 0:DK].astype(BF16)
            st_send[i + 1, :, DK:] = new_b.astype(BF16)
            if i < 2:
                net.start(levels[i + 1])
            else:
                @pl.when((ctx // 32) % 2 == 0)
                def _():
                    levels[3].start()
            relay[...] = jnp.where(upper, r[DK:, 0:DK], old)

            @pl.when(upper)
            def _():
                add_level(i, r[DK:, DK:])

            if i == 0:
                w_pass_on(3)
        else:
            @pl.when(upper)
            def _():
                levels[3].wait_recv()
                add_level(3, dot3(relay[...], st_recv[3, :, DK:].astype(F32)))

            @pl.when(jnp.logical_not(upper))
            def _():
                levels[3].wait_send()

    mine = mt.at[pl.ds(pl.multiple_of(yl * DK, DK), DK)]
    mine[...] = ot[...].astype(BF16)
    o_copies = []
    for d in (3, 2, 1):
        cp = pltpu.make_async_remote_copy(
            src_ref=mine, dst_ref=mine, send_sem=o_ss.at[d], recv_sem=o_rs.at[d],
            device_id={"ctx": base + (yl + d) % 4}, device_id_type=MESH,
        )
        net.start(cp)
        o_copies.append(cp)
    net.arrive(*w_ring[3])
    net.arrive(*o_copies)

    def share(block):
        w = wg[block].reshape(128, 512)
        return jnp.dot(w, mt[...], preferred_element_type=F32)

    sib, xs = {}, []

    def to_sibling(d):
        sib_send[d] = share(((xi + d) % 4) * 2 + 1 - core).astype(BF16)
        sib[d] = pltpu.make_async_remote_copy(
            src_ref=sib_send.at[d], dst_ref=sib_recv.at[d], send_sem=sb_ss.at[d], recv_sem=sb_rs.at[d],
            device_id={"head": head ^ 1}, device_id_type=MESH,
        )
        net.start(sib[d])

    def chip_sum(d):
        own = share(((xi + d) % 4) * 2 + core)
        net.arrive(sib[d])
        return own + sib_recv[d].astype(F32)

    def to_chip(d):
        x_send[d] = chip_sum(d).astype(BF16)
        cp = pltpu.make_async_remote_copy(
            src_ref=x_send.at[d], dst_ref=x_recv.at[d], send_sem=x_ss.at[d], recv_sem=x_rs.at[d],
            device_id={"head": ((xi + d) % 4) * 2 + core}, device_id_type=MESH,
        )
        net.start(cp)
        xs.append((d, cp))

    to_sibling(2)
    to_sibling(1)
    to_chip(2)
    to_sibling(3)
    to_chip(1)
    to_sibling(0)
    to_chip(3)
    total = chip_sum(0)
    for d, cp in xs:
        net.arrive(cp)
        total = total + x_recv[d].astype(F32)

    fsend[...] = total.astype(BF16)
    fcopies = []
    for d in (3, 2, 1):
        cp = pltpu.make_async_remote_copy(
            src_ref=fsend.at[:, lane((yl + d) % 4)], dst_ref=fin.at[yl],
            send_sem=f_ss.at[d], recv_sem=f_rs.at[d],
            device_id={"ctx": base + (yl + d) % 4}, device_id_type=MESH,
        )
        net.start(cp)
        fcopies.append(cp)
    fin[yl] = fsend[:, lane(yl)]
    net.arrive(*fcopies)
    parts = [fin[j, 64 * m : 64 * m + 64, :] for m in range(2) for j in range(4)]
    out_ref[...] = jnp.concatenate(parts, axis=0).astype(F32).T.astype(BF16)

    net.finish()


def per_device(q, k, v, dec, beta, lw, w):
    vmem = pl.BlockSpec(memory_space=pltpu.VMEM)
    dma = pltpu.SemaphoreType.DMA
    return pl.pallas_call(
        kernel,
        out_shape=jax.ShapeDtypeStruct((TB, 512), BF16),
        in_specs=[pl.BlockSpec(memory_space=pltpu.HBM)] * 7,
        out_specs=vmem,
        scratch_shapes=[
            pltpu.VMEM((4, TB), F32),
            pltpu.VMEM((4, TB), F32),
            pltpu.VMEM((7, 4, TB), F32),
            pltpu.VMEM((4, 16, TB), F32),
            pltpu.VMEM((4, TB, DK), BF16),
            pltpu.VMEM((4, TB, DK), BF16),
            pltpu.VMEM((4, TB, DK), BF16),
            pltpu.VMEM((4, 16, TB), F32),
            pltpu.VMEM((4, TB, DK), F32),
            pltpu.VMEM((4, TB, TB), F32),
            pltpu.VMEM((4, TB, 2 * DK), F32),
            pltpu.VMEM((4, DK, 2 * DK), F32),
            pltpu.VMEM((4, TB, DK), F32),
            pltpu.VMEM((DK, 4 * TB), F32),
            pltpu.VMEM((DK, 4 * TB), F32),
            pltpu.VMEM((DK, 2 * DK), F32),
            pltpu.VMEM((DK, DK), F32),
            pltpu.VMEM((4, DK, 2 * DK), BF16),
            pltpu.VMEM((4, DK, 2 * DK), BF16),
            pltpu.VMEM((4 * DK, 4 * TB), BF16),
            pltpu.VMEM((8, 2, 64, 512), BF16),
            pltpu.VMEM((4, DK, 4 * TB), BF16),
            pltpu.VMEM((4, DK, 4 * TB), BF16),
            pltpu.VMEM((4, DK, 4 * TB), BF16),
            pltpu.VMEM((4, DK, 4 * TB), BF16),
            pltpu.VMEM((DK, 4 * TB), BF16),
            pltpu.VMEM((4, DK, TB), BF16),
            dma((3, 4)), dma((3, 4)), dma((4,)), dma((4,)), dma((4,)), dma((4,)),
            dma((4,)), dma((4,)), dma, dma, dma((2, 5)), dma((2, 5)),
            dma((4,)), dma((4,)), dma((4,)), dma((4,)), dma((4,)), dma((4,)), dma((7,)),
        ],
        compiler_params=pltpu.CompilerParams(
            collective_id=0, has_side_effects=True, vmem_limit_bytes=60 * 2**20
        ),
        name="mixer",
    )(q, k, v, dec.T, beta.T, lw.transpose(2, 1, 0), w.T)


def solution(mesh):
    spec = P("ctx", "head")
    return jax.shard_map(
        per_device,
        mesh=mesh,
        in_specs=(spec,) * 5 + (P("ctx", "head", None), P("head", "ctx")),
        out_specs=spec,
        check_vma=False,
    )
```

time: 81.3 us -> 74.5 us (0.916)
  Pallas kernels: 77.3 us -> 72.8 us
  local copies, waits for them, and re-layouts: 3.71 us -> 1.57 us
    pallas_call x1, Pallas kernels: 77.3 us -> 72.8 us  [per_device(): pl.pallas_call(kernel, out_shape=jax.ShapeDtypeStruct((TB, 512), BF16), i...]
    unnamed x17 -> x1, local copies, waits for them, and re-layouts: 3.6 us -> 1.57 us
where the time goes in v2:
time: 74.5 us; the launch traced here: 74.4 us
  Pallas kernels  72.8 us (98%)
  local copies, waits for them, and re-layouts  1.57 us (2%)
    pallas_call x1, Pallas kernels, per_device(): pl.pallas_call(kernel, out_shape=jax.ShapeDtypeStruct((TB, 512), BF16), i...  72.8 us
    unnamed x1, local copies, waits for them, and re-layouts  1.57 us

profile of v2, /device:TPU:1, one launch (start us, length us, event | category | flops | bytes accessed | tf_op | source)
XLA Modules:
  0.0 74.4 jit_solution(16650529067681585654)
XLA Ops:
  0.0 72.8 %mixer.1 = bf16[128,512]{1,0:T(8,128)(2,1)} custom-call(bf16[128,512]{1,0:T(8,128)(2,1)} %q_ref.1, bf16[128,512]{1,0:T(8,128)(2,1)} %k_ref.1, bf16[128,512]{1,0:T(8,128)(2,1)} %v_ref.1, f32[4,128]{1,0:T(4,128)} %bitcast.6, f32[4,128]{1,0:T(4,128)} %bitcast.7, f32[7,4,128]{2,1,0:T(4,128)} %bitcast.5, bf16[64,512]{1,0:T(8,128)(2,1)} %bitcast.4), custom_call_target="tpu_custom_call" | custom-call | tf_op jit(solution)/shard_map/mixer/pallas_call | solution.py:408
  72.8 1.6 %copy.9 = bf16[128,512]{1,0:T(8,128)(2,1)} copy(bf16[128,512]{1,0:T(8,128)(2,1)} %mixer.1) | data formatting | bytes 262144

commit v3 on v2

--- a/solution.py
+++ b/solution.py
@@ -67,10 +67,10 @@
 
 
 def kernel(
-    q_ref, k_ref, v_ref, dec_hbm, beta_hbm, lw_hbm, w_ref, out_ref,
-    dec_ref, beta_ref, lw_ref, small, rq, rk, rv, rs, kn, gm, wu, ab, cols, lrt, ot, tot, relay,
+    q_hbm, k_hbm, v_hbm, dec_hbm, beta_hbm, lw_hbm, w_ref, out_ref,
+    q_ref, k_ref, v_ref, dec_ref, beta_ref, lw_ref, small, rq, rk, rv, rs, kn, gm, wu, ab, cols, lrt, ot, tot, relay,
     st_send, st_recv, mt, wg, sib_send, sib_recv, x_send, x_recv, fsend, fin,
-    kv_ss, kv_rs, q_ss, q_rs, st_ss, st_rs, o_ss, o_rs, w1_ss, w1_rs, w2_ss, w2_rs,
+    kv_ss, kv_rs, st_ss, st_rs, o_ss, o_rs, w1_ss, w1_rs, w2_ss, w2_rs,
     sb_ss, sb_rs, x_ss, x_rs, f_ss, f_rs, in_s,
 ):
     net = Copies()
@@ -90,32 +90,31 @@
     def lane(j):
         return pl.ds(pl.multiple_of(j * DK, DK), DK)
 
+    barrier = pltpu.get_barrier_semaphore()
+    for z in ((zi + 1) % 8, (zi + 7) % 8, zi ^ 2, zi ^ 4):
+        pl.semaphore_signal(barrier, inc=1, device_id=at_zy(z, yi), device_id_type=MESH)
+    pl.semaphore_signal(barrier, inc=1, device_id={"ctx": ctx ^ 4}, device_id_type=MESH)
+    for d in range(1, 4):
+        pl.semaphore_signal(
+            barrier, inc=1, device_id={"ctx": base + (yl + d) % 4}, device_id_type=MESH
+        )
+    for d in (1, 3):
+        pl.semaphore_signal(
+            barrier, inc=1, device_id={"head": ((xi + d) % 4) * 2 + core}, device_id_type=MESH
+        )
+    pl.semaphore_signal(barrier, inc=1, device_id={"head": head ^ 1}, device_id_type=MESH)
+
     loads = [
         pltpu.make_async_copy(src, dst, in_s.at[i])
         for i, (src, dst) in enumerate(
             (
                 (dec_hbm, dec_ref), (beta_hbm, beta_ref), (lw_hbm, lw_ref),
-                (w_ref, wg.at[zi, yh]), (k_ref.at[:, lane(yl)], rk.at[yl]),
-                (v_ref.at[:, lane(yl)], rv.at[yl]), (q_ref.at[:, lane(yl)], rq.at[yl]),
+                (w_ref, wg.at[zi, yh]), (k_hbm, k_ref), (v_hbm, v_ref), (q_hbm, q_ref),
             )
         )
     ]
     for cp in loads:
         cp.start()
-
-    barrier = pltpu.get_barrier_semaphore()
-    for d in range(1, 8):
-        pl.semaphore_signal(barrier, inc=1, device_id=at_zy((zi + d) % 8, yi), device_id_type=MESH)
-    pl.semaphore_signal(barrier, inc=1, device_id={"ctx": ctx ^ 4}, device_id_type=MESH)
-    for d in range(1, 4):
-        pl.semaphore_signal(
-            barrier, inc=1, device_id={"ctx": base + (yl + d) % 4}, device_id_type=MESH
-        )
-    for d in range(1, 4):
-        pl.semaphore_signal(
-            barrier, inc=1, device_id={"head": ((xi + d) % 4) * 2 + core}, device_id_type=MESH
-        )
-    pl.semaphore_signal(barrier, inc=1, device_id={"head": head ^ 1}, device_id_type=MESH)
 
     for cp in loads[:3]:
         cp.wait()
@@ -126,54 +125,68 @@
             small[j, 2 + l : 3 + l, :] = lw_ref[l, j : j + 1]
         small[j, 9:16, :] = jnp.zeros((7, TB), F32)
 
-    pl.semaphore_wait(barrier, 15)
-
-    kv_copies = []
-    for d in (3, 2, 1):
-        to = (yl + d) % 4
-        for a, (src, dst) in enumerate(
-            ((k_ref.at[:, lane(to)], rk), (v_ref.at[:, lane(to)], rv), (small.at[to], rs))
-        ):
-            cp = pltpu.make_async_remote_copy(
-                src_ref=src, dst_ref=dst.at[yl], send_sem=kv_ss.at[a, d], recv_sem=kv_rs.at[a, d],
-                device_id={"ctx": base + to}, device_id_type=MESH,
+    for cp in loads[3:]:
+        cp.wait()
+    pl.semaphore_wait(barrier, 11)
+
+    def to_group(src, dst, a):
+        copies = []
+        for d in (3, 2, 1):
+            to = (yl + d) % 4
+            copies.append(
+                pltpu.make_async_remote_copy(
+                    src_ref=src.at[to] if a == 1 else src.at[:, lane(to)],
+                    dst_ref=dst.at[yl], send_sem=kv_ss.at[a, d], recv_sem=kv_rs.at[a, d],
+                    device_id={"ctx": base + to}, device_id_type=MESH,
+                )
             )
-            net.start(cp)
-            kv_copies.append(cp)
-
-    loads[3].wait()
+        net.start(*copies)
+        return copies
+
+    k_copies = to_group(k_ref, rk, 0)
+    s_copies = to_group(small, rs, 1)
+    v_copies = to_group(v_ref, rv, 2)
+
     w_pair = pltpu.make_async_remote_copy(
         src_ref=wg.at[zi, yh], dst_ref=wg.at[zi, yh], send_sem=w1_ss, recv_sem=w1_rs,
         device_id={"ctx": ctx ^ 4}, device_id_type=MESH,
     )
     net.start(w_pair)
 
-    def w_copy(way, step):
+    def w_copy(sub, way, step):
         slot = (zi + (step - 1) * (2 * way - 1) + 8) % 8
-        part = wg.at[slot] if step < 4 else wg.at[slot, way]
+        part = wg.at[slot, yh if sub == 0 else 1 - yh]
+        if step == 4:
+            part = part.at[pl.ds(32 * way, 32)]
         return pltpu.make_async_remote_copy(
-            src_ref=part, dst_ref=part, send_sem=w2_ss.at[way, step], recv_sem=w2_rs.at[way, step],
+            src_ref=part, dst_ref=part,
+            send_sem=w2_ss.at[sub, way, step], recv_sem=w2_rs.at[sub, way, step],
             device_id=at_zy((zi + 1 + 6 * way) % 8, yi), device_id_type=MESH,
         )
 
-    w_ring = [[w_copy(way, step) for way in range(2)] for step in range(1, 5)]
-
-    def w_pass_on(step):
-        net.arrive(*w_ring[step - 1])
-        net.start(*w_ring[step])
+    w_ring = [
+        [[w_copy(sub, way, step) for way in range(2)] for step in range(1, 5)] for sub in range(2)
+    ]
+
+    def w_pass_on(sub, step):
+        net.arrive(*w_ring[sub][step - 1])
+        net.start(*w_ring[sub][step])
+
+    net.start(*w_ring[0][0])
 
     rs[yl] = small[yl]
-    for cp in loads[4:]:
-        cp.wait()
+    rk[yl] = k_ref[:, lane(yl)]
+    rv[yl] = v_ref[:, lane(yl)]
+    rq[yl] = q_ref[:, lane(yl)]
 
     ri = lax.broadcasted_iota(jnp.int32, (TB, TB), 0)
     ci = lax.broadcasted_iota(jnp.int32, (TB, TB), 1)
     eye = (ri == ci).astype(F32)
     upto = (ri <= ci).astype(F32)
 
-    def pairs(slots):
+    def pairs(slots, values_here=None):
         n = len(slots)
-        ls, rhs, keys, tails, lasts = [], [], [], [], []
+        ls, keys, betas, tails, lasts = [], [], [], [], []
         for s in slots:
             sm = rs[s]
             g_rows = -jnp.dot(
@@ -192,9 +205,8 @@
             gm[s] = ratio
             cols[s] = jnp.broadcast_to(growth, (TB, DK))
             ls.append(jnp.where(ci < ri, b_col * ratio * dot3_nt(kk, kk), 0.0))
-            rhs.append(
-                jnp.concatenate([(b_col * growth) * kk, b_col * rv[s].astype(F32)], axis=1)
-            )
+            keys.append((b_col * growth) * kk)
+            betas.append(b_col)
             tails.append(jnp.exp(g_last - g_col) * kk)
             lasts.append(jnp.exp(g_last))
         inv = [eye - jnp.where((ri % 2 == 1) & (ci == ri - 1), l, 0.0) for l in ls]
@@ -204,7 +216,15 @@
             mid = [dot3(inv[i], jnp.where(mask, ls[i], 0.0)) for i in range(n)]
             inv = [inv[i] - dot3(mid[i], inv[i]) for i in range(n)]
             b *= 2
-        sol = [dot3(inv[i], rhs[i]) for i in range(n)]
+        if values_here is not None:
+            values_here()
+        sol = [
+            dot3(
+                inv[i],
+                jnp.concatenate([keys[i], betas[i] * rv[s].astype(F32)], axis=1),
+            )
+            for i, s in enumerate(slots)
+        ]
         for i, s in enumerate(slots):
             wu[s] = sol[i]
             m = dot3(tails[i].T, sol[i])
@@ -212,22 +232,16 @@
             ab[s, :, DK:] = m[:, DK:]
 
     pairs([yl])
+    w_pass_on(0, 1)
     net.arrive(w_pair)
-    net.start(*w_ring[0])
-
-    net.arrive(*kv_copies)
-    q_copies = []
-    for d in (3, 2, 1):
-        to = (yl + d) % 4
-        cp = pltpu.make_async_remote_copy(
-            src_ref=q_ref.at[:, lane(to)], dst_ref=rq.at[yl], send_sem=q_ss.at[d], recv_sem=q_rs.at[d],
-            device_id={"ctx": base + to}, device_id_type=MESH,
-        )
-        net.start(cp)
-        q_copies.append(cp)
-    w_pass_on(1)
-
-    pairs([(yl + d) % 4 for d in range(1, 4)])
+    net.start(*w_ring[1][0])
+
+    net.arrive(*s_copies)
+    net.arrive(*k_copies)
+    q_copies = to_group(q_ref, rq, 3)
+    w_pass_on(0, 2)
+
+    pairs([(yl + d) % 4 for d in range(1, 4)], lambda: net.arrive(*v_copies))
 
     def apply(second, first):
         r = dot3(second[:, 0:DK], first)
@@ -252,6 +266,8 @@
     st_send[0] = group.astype(BF16)
     net.start(levels[0])
     relay[...] = eye
+    w_pass_on(1, 1)
+    w_pass_on(0, 3)
 
     net.arrive(*q_copies)
     b01 = ab01[:, DK:]
@@ -290,7 +306,7 @@
             sl = slice(s * TB, (s + 1) * TB)
             ot[:, sl] = ot[:, sl] + rs[s, 4 + i + 1 : 4 + i + 2, :] * t[:, sl]
 
-    w_pass_on(2)
+    w_pass_on(1, 2)
 
     for i in range(4):
         upper = (ctx // (4 << i)) % 2 == 1
@@ -320,7 +336,7 @@
                 add_level(i, r[DK:, DK:])
 
             if i == 0:
-                w_pass_on(3)
+                w_pass_on(1, 3)
         else:
             @pl.when(upper)
             def _():
@@ -341,7 +357,8 @@
         )
         net.start(cp)
         o_copies.append(cp)
-    net.arrive(*w_ring[3])
+    net.arrive(*w_ring[0][3])
+    net.arrive(*w_ring[1][3])
     net.arrive(*o_copies)
 
     def share(block):
@@ -363,26 +380,44 @@
         net.arrive(sib[d])
         return own + sib_recv[d].astype(F32)
 
-    def to_chip(d):
-        x_send[d] = chip_sum(d).astype(BF16)
-        cp = pltpu.make_async_remote_copy(
-            src_ref=x_send.at[d], dst_ref=x_recv.at[d], send_sem=x_ss.at[d], recv_sem=x_rs.at[d],
-            device_id={"head": ((xi + d) % 4) * 2 + core}, device_id_type=MESH,
-        )
-        net.start(cp)
-        xs.append((d, cp))
+    def x_copy(i, src, way):
+        return pltpu.make_async_remote_copy(
+            src_ref=src, dst_ref=x_recv.at[i], send_sem=x_ss.at[i], recv_sem=x_rs.at[i],
+            device_id={"head": ((xi + 1 + 2 * way) % 4) * 2 + core}, device_id_type=MESH,
+        )
+
+    halves = (pl.ds(0, 64), pl.ds(64, 64))
+    x_far = [x_copy(way, x_send.at[2, halves[way]], way) for way in range(2)]
+    x_plain = [x_copy(2 + way, x_send.at[1 + 2 * way, halves[1 - way]], way) for way in range(2)]
+    x_added = [x_copy(4 + way, x_send.at[1 + 2 * way, halves[way]], way) for way in range(2)]
+
+    def to_neighbour(way):
+        near = chip_sum(1 + 2 * way)
+        keep, add = (near[64:], near[:64]) if way == 0 else (near[:64], near[64:])
+        x_send[1 + 2 * way, halves[1 - way], :] = keep.astype(BF16)
+        net.start(x_plain[way])
+        return add
+
+    def pass_added(way, add):
+        net.arrive(x_far[way])
+        x_send[1 + 2 * way, halves[way], :] = (add + x_recv[way].astype(F32)).astype(BF16)
+        net.start(x_added[way])
 
     to_sibling(2)
     to_sibling(1)
-    to_chip(2)
+    x_send[2] = chip_sum(2).astype(BF16)
+    net.start(*x_far)
     to_sibling(3)
-    to_chip(1)
+    add0 = to_neighbour(0)
     to_sibling(0)
-    to_chip(3)
+    add1 = to_neighbour(1)
+    pass_added(0, add0)
+    pass_added(1, add1)
     total = chip_sum(0)
-    for d, cp in xs:
-        net.arrive(cp)
-        total = total + x_recv[d].astype(F32)
+    net.arrive(*x_plain, *x_added)
+    low = x_recv[3].astype(F32) + x_recv[4].astype(F32)
+    high = x_recv[2].astype(F32) + x_recv[5].astype(F32)
+    total = total + jnp.concatenate([low, high], axis=0)
 
     fsend[...] = total.astype(BF16)
     fcopies = []
@@ -411,6 +446,9 @@
         in_specs=[pl.BlockSpec(memory_space=pltpu.HBM)] * 7,
         out_specs=vmem,
         scratch_shapes=[
+            pltpu.VMEM((TB, 4 * DK), BF16),
+            pltpu.VMEM((TB, 4 * DK), BF16),
+            pltpu.VMEM((TB, 4 * DK), BF16),
             pltpu.VMEM((4, TB), F32),
             pltpu.VMEM((4, TB), F32),
             pltpu.VMEM((7, 4, TB), F32),
@@ -435,12 +473,12 @@
             pltpu.VMEM((4, DK, 4 * TB), BF16),
             pltpu.VMEM((4, DK, 4 * TB), BF16),
             pltpu.VMEM((4, DK, 4 * TB), BF16),
-            pltpu.VMEM((4, DK, 4 * TB), BF16),
+            pltpu.VMEM((6, 64, 4 * TB), BF16),
             pltpu.VMEM((DK, 4 * TB), BF16),
             pltpu.VMEM((4, DK, TB), BF16),
-            dma((3, 4)), dma((3, 4)), dma((4,)), dma((4,)), dma((4,)), dma((4,)),
-            dma((4,)), dma((4,)), dma, dma, dma((2, 5)), dma((2, 5)),
-            dma((4,)), dma((4,)), dma((4,)), dma((4,)), dma((4,)), dma((4,)), dma((7,)),
+            dma((4, 4)), dma((4, 4)), dma((4,)), dma((4,)),
+            dma((4,)), dma((4,)), dma, dma, dma((2, 2, 5)), dma((2, 2, 5)),
+            dma((4,)), dma((4,)), dma((6,)), dma((6,)), dma((4,)), dma((4,)), dma((7,)),
         ],
         compiler_params=pltpu.CompilerParams(
             collective_id=0, has_side_effects=True, vmem_limit_bytes=60 * 2**20

time: 74.5 us -> 70.2 us (0.942)
  Pallas kernels: 72.8 us -> 68.5 us
    pallas_call x1, Pallas kernels: 72.8 us -> 68.5 us  [per_device(): pl.pallas_call(kernel, out_shape=jax.ShapeDtypeStruct((TB, 512), BF16), i...]
where the time goes in v3:
time: 70.2 us; the launch traced here: 70.1 us
  Pallas kernels  68.5 us (98%)
  local copies, waits for them, and re-layouts  1.57 us (2%)
    pallas_call x1, Pallas kernels, per_device(): pl.pallas_call(kernel, out_shape=jax.ShapeDtypeStruct((TB, 512), BF16), i...  68.5 us
    unnamed x1, local copies, waits for them, and re-layouts  1.57 us

profile of v3, /device:TPU:1, one launch (start us, length us, event | category | flops | bytes accessed | tf_op | source)
XLA Modules:
  0.0 70.1 jit_solution(3960862211306083164)
XLA Ops:
  0.0 68.5 %mixer.1 = bf16[128,512]{1,0:T(8,128)(2,1)} custom-call(bf16[128,512]{1,0:T(8,128)(2,1)} %q_hbm.1, bf16[128,512]{1,0:T(8,128)(2,1)} %k_hbm.1, bf16[128,512]{1,0:T(8,128)(2,1)} %v_hbm.1, f32[4,128]{1,0:T(4,128)} %bitcast.6, f32[4,128]{1,0:T(4,128)} %bitcast.7, f32[7,4,128]{2,1,0:T(4,128)} %bitcast.5, bf16[64,512]{1,0:T(8,128)(2,1)} %bitcast.4), custom_call_target="tpu_custom_call" | custom-call | tf_op jit(solution)/shard_map/mixer/pallas_call | solution.py:443
  68.5 1.6 %copy.9 = bf16[128,512]{1,0:T(8,128)(2,1)} copy(bf16[128,512]{1,0:T(8,128)(2,1)} %mixer.1) | data formatting | bytes 262144

commit v4 on v3

--- a/solution.py
+++ b/solution.py
@@ -233,15 +233,18 @@
 
     pairs([yl])
     w_pass_on(0, 1)
-    net.arrive(w_pair)
-    net.start(*w_ring[1][0])
 
     net.arrive(*s_copies)
     net.arrive(*k_copies)
     q_copies = to_group(q_ref, rq, 3)
     w_pass_on(0, 2)
 
-    pairs([(yl + d) % 4 for d in range(1, 4)], lambda: net.arrive(*v_copies))
+    def values_here():
+        net.arrive(*v_copies)
+        net.arrive(w_pair)
+        net.start(*w_ring[1][0])
+
+    pairs([(yl + d) % 4 for d in range(1, 4)], values_here)
 
     def apply(second, first):
         r = dot3(second[:, 0:DK], first)
@@ -300,13 +303,11 @@
         lrt[:, s * TB : (s + 1) * TB] = lifted.T
         ot[:, s * TB : (s + 1) * TB] = o
 
-    def add_level(i, state):
-        t = dot3(state.T, lrt[...])
+    def add_level(i, state, lifted=None):
+        t = dot3(state.T, lrt[...] if lifted is None else lifted)
         for s in range(4):
             sl = slice(s * TB, (s + 1) * TB)
             ot[:, sl] = ot[:, sl] + rs[s, 4 + i + 1 : 4 + i + 2, :] * t[:, sl]
-
-    w_pass_on(1, 2)
 
     for i in range(4):
         upper = (ctx // (4 << i)) % 2 == 1
@@ -335,13 +336,14 @@
             def _():
                 add_level(i, r[DK:, DK:])
 
-            if i == 0:
-                w_pass_on(1, 3)
+            if i < 2:
+                w_pass_on(1, 2 + i)
         else:
             @pl.when(upper)
             def _():
+                lifted = dot3(relay[...].T, lrt[...])
                 levels[3].wait_recv()
-                add_level(3, dot3(relay[...], st_recv[3, :, DK:].astype(F32)))
+                add_level(3, st_recv[3, :, DK:].astype(F32), lifted)
 
             @pl.when(jnp.logical_not(upper))
             def _():
@@ -403,13 +405,11 @@
         x_send[1 + 2 * way, halves[way], :] = (add + x_recv[way].astype(F32)).astype(BF16)
         net.start(x_added[way])
 
-    to_sibling(2)
-    to_sibling(1)
+    for d in (2, 1, 3, 0):
+        to_sibling(d)
     x_send[2] = chip_sum(2).astype(BF16)
     net.start(*x_far)
-    to_sibling(3)
     add0 = to_neighbour(0)
-    to_sibling(0)
     add1 = to_neighbour(1)
     pass_added(0, add0)
     pass_added(1, add1)

time: 70.2 us -> 68.1 us (0.970); the launches traced: 70.1 us -> 67.2 us
  Pallas kernels: 68.5 us -> 65.7 us
    pallas_call x1, Pallas kernels: 68.5 us -> 65.7 us  [per_device(): pl.pallas_call(kernel, out_shape=jax.ShapeDtypeStruct((TB, 512), BF16), i...]
where the time goes in v4:
time: 68.1 us; the launch traced here: 67.2 us
  Pallas kernels  65.7 us (96%)
  local copies, waits for them, and re-layouts  1.57 us (2%)
    pallas_call x1, Pallas kernels, per_device(): pl.pallas_call(kernel, out_shape=jax.ShapeDtypeStruct((TB, 512), BF16), i...  65.7 us
    unnamed x1, local copies, waits for them, and re-layouts  1.57 us

profile of v4, /device:TPU:1, one launch (start us, length us, event | category | flops | bytes accessed | tf_op | source)
XLA Modules:
  0.0 67.2 jit_solution(6657238238905807654)
XLA Ops:
  0.0 65.7 %mixer.1 = bf16[128,512]{1,0:T(8,128)(2,1)} custom-call(bf16[128,512]{1,0:T(8,128)(2,1)} %q_hbm.1, bf16[128,512]{1,0:T(8,128)(2,1)} %k_hbm.1, bf16[128,512]{1,0:T(8,128)(2,1)} %v_hbm.1, f32[4,128]{1,0:T(4,128)} %bitcast.6, f32[4,128]{1,0:T(4,128)} %bitcast.7, f32[7,4,128]{2,1,0:T(4,128)} %bitcast.5, bf16[64,512]{1,0:T(8,128)(2,1)} %bitcast.4), custom_call_target="tpu_custom_call" | custom-call | tf_op jit(solution)/shard_map/mixer/pallas_call | solution.py:443
  65.7 1.6 %copy.9 = bf16[128,512]{1,0:T(8,128)(2,1)} copy(bf16[128,512]{1,0:T(8,128)(2,1)} %mixer.1) | data formatting | bytes 262144

commit v5 on v4

--- a/solution.py
+++ b/solution.py
@@ -411,9 +411,9 @@
     net.start(*x_far)
     add0 = to_neighbour(0)
     add1 = to_neighbour(1)
+    total = chip_sum(0)
     pass_added(0, add0)
     pass_added(1, add1)
-    total = chip_sum(0)
     net.arrive(*x_plain, *x_added)
     low = x_recv[3].astype(F32) + x_recv[4].astype(F32)
     high = x_recv[2].astype(F32) + x_recv[5].astype(F32)

time: 68.1 us -> 68.1 us (level)
  no operation moved by 1% of the time
where the time goes in v5:
time: 68.1 us; the launch traced here: 67.2 us
  Pallas kernels  65.7 us (96%)
  local copies, waits for them, and re-layouts  1.57 us (2%)
    pallas_call x1, Pallas kernels, per_device(): pl.pallas_call(kernel, out_shape=jax.ShapeDtypeStruct((TB, 512), BF16), i...  65.7 us
    unnamed x1, local copies, waits for them, and re-layouts  1.57 us

profile of v5, /device:TPU:1, one launch (start us, length us, event | category | flops | bytes accessed | tf_op | source)
XLA Modules:
  0.0 67.2 jit_solution(16291883493090299592)
XLA Ops:
  0.0 65.7 %mixer.1 = bf16[128,512]{1,0:T(8,128)(2,1)} custom-call(bf16[128,512]{1,0:T(8,128)(2,1)} %q_hbm.1, bf16[128,512]{1,0:T(8,128)(2,1)} %k_hbm.1, bf16[128,512]{1,0:T(8,128)(2,1)} %v_hbm.1, f32[4,128]{1,0:T(4,128)} %bitcast.6, f32[4,128]{1,0:T(4,128)} %bitcast.7, f32[7,4,128]{2,1,0:T(4,128)} %bitcast.5, bf16[64,512]{1,0:T(8,128)(2,1)} %bitcast.4), custom_call_target="tpu_custom_call" | custom-call | tf_op jit(solution)/shard_map/mixer/pallas_call | solution.py:443
  65.7 1.6 %copy.9 = bf16[128,512]{1,0:T(8,128)(2,1)} copy(bf16[128,512]{1,0:T(8,128)(2,1)} %mixer.1) | data formatting | bytes 262144
